TPU v7x, 512 devices: a whole 4x4x16 slice. The times are simulated.
512 devices in a mesh: batch: 16 (over z_hi, y, core), tensor: 32 (over x, z_lo).
Axes of the slice: x: 4, y: 4, z: 16 (z_hi: 2, z_lo: 8; z = z_hi * 8 + z_lo), core: 2. Of those that a mesh axis runs over, the one named last changes fastest.
Arguments:
- tokens: bfloat16 [4096, 4096], P('batch', 'tensor'), may hold values from -6 to 6
- gate_pre: bfloat16 [4096, 14336], P('batch', 'tensor'), may hold values from -8 to 8
- up_pre: bfloat16 [4096, 14336], P('batch', 'tensor'), may hold values from -6 to 6
- down_weight: bfloat16 [14336, 4096], P('tensor'), may hold values from -0.046875 to 0.046875
- tangent_gate: bfloat16 [4096, 14336], P('batch', 'tensor'), may hold values from -0.09375 to 0.09375
- loss_weight: float32 [4096], P('batch'), may hold values from 0.05 to 0.5
Outputs:
- gnvp: float32 [4096, 14336], P('batch', 'tensor')
All inputs are finite; a program needn't handle non-finite values.
Results may differ from a plain program's by a relative error of at most 0.025.
Values may be sent and summed in bfloat16 or wider, within the bound.
A program may use at most 64 MiB of HBM per device.

v0:
```python
import jax
import jax.numpy as jnp
from jax import lax
from jax.sharding import PartitionSpec as P


def slope_of(gate_pre, up_pre):
    a = gate_pre.astype(jnp.float32)
    sig = jax.nn.sigmoid(a)
    return sig * (1.0 + a * (1.0 - sig)) * up_pre.astype(jnp.float32)


def body(tokens, gate_pre, up_pre, down_weight, tangent_gate, loss_weight):
    whole = lax.all_gather(tokens, "tensor", axis=1, tiled=True)
    slope = slope_of(gate_pre, up_pre)
    columns = whole
    tangent_gate_out = jnp.dot(
        columns,
        lax.all_gather(tangent_gate, "batch", axis=0, tiled=True),
        preferred_element_type=jnp.float32,
    )
    tangent_hidden = (slope * tangent_gate_out).astype(jnp.bfloat16)
    partial_out = jnp.dot(tangent_hidden, down_weight, preferred_element_type=jnp.float32)
    tangent_out = lax.psum(partial_out.astype(jnp.bfloat16), "tensor").astype(jnp.float32)
    weighted = (loss_weight[:, None] * tangent_out).astype(jnp.bfloat16)
    back_hidden = jnp.einsum("td,fd->tf", weighted, down_weight, preferred_element_type=jnp.float32)
    back_gate = (back_hidden * slope).astype(jnp.bfloat16)
    columns = whole
    return lax.psum_scatter(
        jnp.einsum("td,tf->df", columns, back_gate, preferred_element_type=jnp.float32).astype(
            jnp.bfloat16
        ),
        "batch",
        scatter_dimension=0,
        tiled=True,
    ).astype(jnp.float32)


def solution(mesh):
    placed = (
        P("batch", "tensor"),
        P("batch", "tensor"),
        P("batch", "tensor"),
        P("tensor", None),
        P("batch", "tensor"),
        P("batch"),
    )
    return jax.shard_map(
        body, mesh=mesh, in_specs=placed, out_specs=P("batch", "tensor"), check_vma=False
    )
```

profile of v0, /device:TPU:2, one launch (start us, length us, event | category | flops | bytes accessed | tf_op | source)
XLA Modules:
  0.0 940.3 jit_solution(17871154214957523726)
XLA Ops:
  6.5 0.0 all-gather.3.cloned.1.call-start
  6.5 0.7 all-gather.3.cloned.1.call-update
  7.3 0.0 all-gather.5.cloned.1.call-start
  7.3 0.7 all-gather.5.cloned.1.call-update
  8.0 0.0 copy-start.1
  8.0 0.0 copy-start.2
  8.0 0.0 copy-start.3
  8.0 0.0 all-reduce.2.cloned.1.call-start
  8.1 183.1 %all-gather.3.cloned.1.call-done = bf16[256,4096]{1,0:T(8,128)(2,1)} async-done(((bf16[256,128]{1,0:T(8,128)(2,1)}), bf16[256,4096]{1,0:T(8,128)(2,1)}) %all-gather.3.cloned.1.call-update) | async-done | bytes 2097168 | tf_op jit(solution)/shard_map/all_gather | solution.py:14
  191.1 0.0 copy-start
  191.1 120.4 %all-gather.5.cloned.1.call-done = bf16[4096,448]{0,1:T(8,128)(2,1)} async-done(((bf16[256,448]{0,1:T(8,128)(2,1)}), bf16[4096,448]{0,1:T(8,128)(2,1)}) %all-gather.5.cloned.1.call-update) | async-done | bytes 3670032 | tf_op jit(solution)/shard_map/all_gather | solution.py:19
  311.5 9.6 %convolution_convert_fusion.1 = bf16[256,4096]{1,0:T(8,128)(2,1)} fusion(bf16[448,4096]{1,0:T(8,128)(2,1)} %param.9, bf16[256,4096]{1,0:T(8,128)(2,1)} %all-gather.3.cloned.1.call-done, bf16[4096,448]{0,1:T(8,128)(2,1)} %all-gather.5.cloned.1.call-done, bf16[256,448]{0,1:T(8,128)(2,1)} %param.7, bf16[256,448]{0,1:T(8,128)(2,1)} %param.8), kind=kOutput, calls=%fused_computation.2 | convolution fusion | flops 1881473024 | bytes 11993088 | tf_op jit(solution)/shard_map/dot_general | solution.py:23
  321.1 0.0 all-reduce.2.cloned.1.call-update
  321.1 0.0 reduce-scatter.2.cloned.1.call-start
  321.2 440.5 %all-reduce.2.cloned.1.call-done = bf16[256,4096]{1,0:T(8,128)(2,1)} async-done(((bf16[256,4096]{1,0:T(8,128)(2,1)}), bf16[256,4096]{1,0:T(8,128)(2,1)}) %all-reduce.2.cloned.1.call-update) | async-done | bytes 2097168 | tf_op jit(solution)/shard_map/psum | solution.py:24
  761.7 0.0 copy-done.1
  761.7 0.0 copy-done.2
  761.7 0.0 copy-done.3
  761.7 0.0 copy-done
  761.7 8.6 fusion
  770.3 0.0 reduce-scatter.2.cloned.1.call-update
  770.3 161.8 %reduce-scatter.2.cloned.1.call-done = bf16[256,448]{0,1:T(8,128)(2,1)} async-done(((bf16[4096,448]{0,1:T(8,128)(2,1)}), bf16[256,448]{0,1:T(8,128)(2,1)}) %reduce-scatter.2.cloned.1.call-update) | async-done | bytes 229392 | tf_op jit(solution)/shard_map/reduce_scatter | solution.py:29
  932.1 1.7 convert_element_type.39
Async XLA Ops:
  6.5 184.6 %all-gather.3.cloned.1.call-start = ((), (), s32[]{:S(2)}) async-start(), calls=%async_computation.1 | async-start | bytes 2162688 | tf_op jit(solution)/shard_map/all_gather | solution.py:14
  7.3 304.3 %all-gather.5.cloned.1.call-start = ((), (), s32[]{:S(2)}) async-start(), calls=%async_computation.2 | async-start | bytes 3899392 | tf_op jit(solution)/shard_map/all_gather | solution.py:19
  8.0 753.7 %copy-start.1 = (bf16[256,448]{0,1:T(8,128)(2,1)S(1)}, bf16[256,448]{0,1:T(8,128)(2,1)}, u32[]{:S(2)}) copy-start(bf16[256,448]{0,1:T(8,128)(2,1)} %param.7) | copy-start | bytes 688132
  8.0 753.7 %copy-start.2 = (bf16[256,448]{0,1:T(8,128)(2,1)S(1)}, bf16[256,448]{0,1:T(8,128)(2,1)}, u32[]{:S(2)}) copy-start(bf16[256,448]{0,1:T(8,128)(2,1)} %param.8) | copy-start | bytes 688132
  8.0 753.7 %copy-start.3 = (f32[256]{0:T(256)S(1)}, f32[256]{0:T(256)}, u32[]{:S(2)}) copy-start(f32[256]{0:T(256)} %param.11) | copy-start | bytes 3076
  8.0 753.6 %all-reduce.2.cloned.1.call-start = ((), (), s32[]{:S(2)}) async-start(), calls=%async_computation.3 | async-start | bytes 4194304 | tf_op jit(solution)/shard_map/psum | solution.py:24
  191.1 570.5 %copy-start = (bf16[256,4096]{1,0:T(8,128)(2,1)S(1)}, bf16[256,4096]{1,0:T(8,128)(2,1)}, u32[]{:S(2)}) copy-start(bf16[256,4096]{1,0:T(8,128)(2,1)} %all-gather.3.cloned.1.call-done) | copy-start | bytes 6291460
  321.1 610.9 %reduce-scatter.2.cloned.1.call-start = ((), (), s32[]{:S(2)}) async-start(), calls=%async_computation.4 | async-start | bytes 3899392 | tf_op jit(solution)/shard_map/reduce_scatter | solution.py:29
Sparse Core Ops, SparseCore 0:
  9.4 181.7 all-gather.2
  194.3 117.2 all-gather.4
  321.2 440.3 all-reduce.1
  770.4 161.6 reduce-scatter.1
where the time goes:
time: 940 us
  waiting for transfers between devices  907 us (96%)
  matrix products  18.1 us (2%)
  between operations  13.2 us (1%)
    psum x1, waiting for transfers between devices, body(): lax.psum(partial_out.astype(jnp.bfloat16), 'tensor').astype(jnp.float32)  441 us
    all_gather x1, waiting for transfers between devices, body(): whole = lax.all_gather(tokens, 'tensor', axis=1, tiled=True)  183 us
    reduce_scatter x1, waiting for transfers between devices, body(): lax.psum_scatter(jnp.einsum('td,tf->df', columns, back_gate, preferred_el...  162 us
    all_gather x1, waiting for transfers between devices, body(): lax.all_gather(tangent_gate, 'batch', axis=0, tiled=True)  120 us
  transfers between devices with their start and end apart: 4, of which 4 were waited for; matrix products, arithmetic and copies ran while one was open for 0% of the time, Pallas kernels for 0%

commit v1 on v0

--- a/solution.py
+++ b/solution.py
@@ -2,6 +2,7 @@
 import jax.numpy as jnp
 from jax import lax
 from jax.sharding import PartitionSpec as P
+from jax.lax import all_to_all, axis_size
 
 
 def slope_of(gate_pre, up_pre):
@@ -14,10 +15,20 @@
     whole = lax.all_gather(tokens, "tensor", axis=1, tiled=True)
     slope = slope_of(gate_pre, up_pre)
     columns = whole
+
+    def map_packet(sheet, in_dim):
+        return jnp.concatenate(
+            all_to_all(
+                jnp.stack([sheet] * axis_size("batch"), axis=0),
+                "batch",
+                split_axis=0,
+                concat_axis=0,
+            ),
+            axis=in_dim,
+        )
+
     tangent_gate_out = jnp.dot(
-        columns,
-        lax.all_gather(tangent_gate, "batch", axis=0, tiled=True),
-        preferred_element_type=jnp.float32,
+        columns, map_packet(tangent_gate, 0), preferred_element_type=jnp.float32
     )
     tangent_hidden = (slope * tangent_gate_out).astype(jnp.bfloat16)
     partial_out = jnp.dot(tangent_hidden, down_weight, preferred_element_type=jnp.float32)

time: 940 us -> 971 us (1.033)
  starting transfers between devices: 0.12 us -> 18 us
    all_gather x1 -> x0, waiting for transfers between devices: 120 us -> none  [body(): lax.all_gather(tangent_gate, 'batch', axis=0, tiled=True)]
    all_to_all x0 -> x1, waiting for transfers between devices: none -> 97.6 us  [map_packet(): all_to_all(jnp.stack([sheet] * axis_size('batch'), axis=0), 'batch', spli...]
    all_gather x1, waiting for transfers between devices: 183 us -> 202 us  [body(): whole = lax.all_gather(tokens, 'tensor', axis=1, tiled=True)]
    all_to_all x0 -> x1, starting transfers between devices: none -> 17.9 us  [map_packet(): all_to_all(jnp.stack([sheet] * axis_size('batch'), axis=0), 'batch', spli...]
    psum x1, waiting for transfers between devices: 441 us -> 451 us  [body(): lax.psum(partial_out.astype(jnp.bfloat16), 'tensor').astype(jnp.float32)]
where the time goes in v1:
time: 971 us
  waiting for transfers between devices  912 us (94%)
  matrix products  18.1 us (2%)
  starting transfers between devices  18 us (2%)
  between operations  13.1 us (1%)
    psum x1, waiting for transfers between devices, body(): lax.psum(partial_out.astype(jnp.bfloat16), 'tensor').astype(jnp.float32)  451 us
    all_gather x1, waiting for transfers between devices, body(): whole = lax.all_gather(tokens, 'tensor', axis=1, tiled=True)  202 us
    reduce_scatter x1, waiting for transfers between devices, body(): lax.psum_scatter(jnp.einsum('td,tf->df', columns, back_gate, preferred_el...  162 us
    all_to_all x1, waiting for transfers between devices, map_packet(): all_to_all(jnp.stack([sheet] * axis_size('batch'), axis=0), 'batch', spli...  97.6 us
  transfers between devices with their start and end apart: 4, of which 4 were waited for; matrix products, arithmetic and copies ran while one was open for 0% of the time, Pallas kernels for 0%

profile of v1, /device:TPU:2, one launch (start us, length us, event | category | flops | bytes accessed | tf_op | source)
XLA Modules:
  0.0 970.8 jit_solution(17477427549754074123)
XLA Ops:
  6.5 3.1 stack.2
  9.6 17.9 %all-to-all-start = ((bf16[16,256,448]{1,2,0:T(8,128)(2,1)}), bf16[16,256,448]{1,2,0:T(8,128)(2,1)}, u32[]{:S(2)}, u32[]{:S(2)}) async-start(bf16[16,256,448]{1,2,0:T(8,128)(2,1)} %stack.2), calls=%async_computation | async-start | bytes 7340032 | tf_op jit(solution)/shard_map/all_to_all | solution.py:21
  27.5 0.0 all-gather.2.cloned.1.call-start
  27.6 0.7 all-gather.2.cloned.1.call-update
  28.3 0.0 all-reduce.2.cloned.1.call-start
  28.3 97.6 %all-to-all-done = bf16[16,256,448]{1,2,0:T(8,128)(2,1)} async-done(((bf16[16,256,448]{1,2,0:T(8,128)(2,1)}), bf16[16,256,448]{1,2,0:T(8,128)(2,1)}, u32[]{:S(2)}, u32[]{:S(2)}) %all-to-all-start) | async-done | bytes 3670048 | tf_op jit(solution)/shard_map/all_to_all | solution.py:21
  125.9 0.0 copy-start.1
  125.9 0.0 copy-start.2
  125.9 4.4 copy.9
  130.3 201.7 %all-gather.2.cloned.1.call-done = bf16[256,4096]{1,0:T(8,128)(2,1)} async-done(((bf16[256,128]{1,0:T(8,128)(2,1)}), bf16[256,4096]{1,0:T(8,128)(2,1)}) %all-gather.2.cloned.1.call-update) | async-done | bytes 2097168 | tf_op jit(solution)/shard_map/all_gather | solution.py:15
  332.0 0.0 copy-done.1
  332.1 0.0 copy-done.2
  332.1 0.0 copy-start
  332.1 0.0 copy-start.3
  332.1 9.5 convolution_convert_fusion.1
  341.6 0.0 all-reduce.2.cloned.1.call-update
  341.6 0.0 reduce-scatter.2.cloned.1.call-start
  341.7 450.5 %all-reduce.2.cloned.1.call-done = bf16[256,4096]{1,0:T(8,128)(2,1)} async-done(((bf16[256,4096]{1,0:T(8,128)(2,1)}), bf16[256,4096]{1,0:T(8,128)(2,1)}) %all-reduce.2.cloned.1.call-update) | async-done | bytes 2097168 | tf_op jit(solution)/shard_map/psum | solution.py:35
  792.2 0.0 copy-done
  792.2 0.0 copy-done.3
  792.2 8.6 fusion
  800.7 0.0 reduce-scatter.2.cloned.1.call-update
  800.8 161.8 %reduce-scatter.2.cloned.1.call-done = bf16[256,448]{0,1:T(8,128)(2,1)} async-done(((bf16[4096,448]{0,1:T(8,128)(2,1)}), bf16[256,448]{0,1:T(8,128)(2,1)}) %reduce-scatter.2.cloned.1.call-update) | async-done | bytes 229392 | tf_op jit(solution)/shard_map/reduce_scatter | solution.py:40
  962.5 1.7 convert_element_type.39
Async XLA Ops:
  9.6 116.2 %all-to-all-start = ((bf16[16,256,448]{1,2,0:T(8,128)(2,1)}), bf16[16,256,448]{1,2,0:T(8,128)(2,1)}, u32[]{:S(2)}, u32[]{:S(2)}) async-start(bf16[16,256,448]{1,2,0:T(8,128)(2,1)} %stack.2), calls=%async_computation | async-start | bytes 7340032 | tf_op jit(solution)/shard_map/all_to_all | solution.py:21
  27.5 304.5 %all-gather.2.cloned.1.call-start = ((), (), s32[]{:S(2)}) async-start(), calls=%async_computation.2 | async-start | bytes 2162688 | tf_op jit(solution)/shard_map/all_gather | solution.py:15
  28.3 763.9 %all-reduce.2.cloned.1.call-start = ((), (), s32[]{:S(2)}) async-start(), calls=%async_computation.3 | async-start | bytes 4194304 | tf_op jit(solution)/shard_map/psum | solution.py:35
  125.9 206.2 %copy-start.1 = (bf16[256,448]{0,1:T(8,128)(2,1)S(1)}, bf16[256,448]{0,1:T(8,128)(2,1)}, u32[]{:S(2)}) copy-start(bf16[256,448]{0,1:T(8,128)(2,1)} %param.7) | copy-start | bytes 688132
  125.9 206.2 %copy-start.2 = (bf16[256,448]{0,1:T(8,128)(2,1)S(1)}, bf16[256,448]{0,1:T(8,128)(2,1)}, u32[]{:S(2)}) copy-start(bf16[256,448]{0,1:T(8,128)(2,1)} %param.8) | copy-start | bytes 688132
  332.1 460.1 %copy-start = (bf16[256,4096]{1,0:T(8,128)(2,1)S(1)}, bf16[256,4096]{1,0:T(8,128)(2,1)}, u32[]{:S(2)}) copy-start(bf16[256,4096]{1,0:T(8,128)(2,1)} %all-gather.2.cloned.1.call-done) | copy-start | bytes 6291460
  332.1 460.1 %copy-start.3 = (f32[256]{0:T(256)S(1)}, f32[256]{0:T(256)}, u32[]{:S(2)}) copy-start(f32[256]{0:T(256)} %param.11) | copy-start | bytes 3076
  341.6 620.9 %reduce-scatter.2.cloned.1.call-start = ((), (), s32[]{:S(2)}) async-start(), calls=%async_computation.4 | async-start | bytes 3899392 | tf_op jit(solution)/shard_map/reduce_scatter | solution.py:40
Sparse Core Ops, SparseCore 0:
  30.4 301.6 all-gather.1
  341.7 450.4 all-reduce.1
  800.9 161.5 reduce-scatter.1
